TPU v7x, 32 devices: a whole 2x2x4 slice. The times are simulated.
32 devices in a mesh: grp: 2 (over y), bin: 4 (over z), blk: 2 (over x), sub: 2 (over core).
Axes of the slice: x: 2, y: 2, z: 4, core: 2. Of those that a mesh axis runs over, the one named last changes fastest.
Arguments:
- band: float32 [16, 8, 256, 256], P(('grp', 'bin', 'blk'), None, None, 'sub'), parts along dimension 0, as said below
- far_tiles: float32 [256, 256, 256], P(('grp', 'bin', 'blk'), None, 'sub'), parts along dimension 0, as said below
- far_list: int32 [256, 2], P(('grp', 'bin', 'blk')), parts along dimension 0, may hold values from 0 to 7, as said below
- far_count: int32 [16], P(('grp', 'bin', 'blk')), parts along dimension 0, may hold values from 1 to 16, as said below
- masked: int32 [256], P(('grp', 'bin')), parts along dimension 0, may hold values from 0 to 2047, as said below
Outputs:
- bias: float32 [4096], P(('grp', 'bin', 'blk')), parts along dimension 0
- coverage: float32 [4096], P(('grp', 'bin', 'blk')), parts along dimension 0
There are 2 independent parts, one for each index of `grp`. A program takes and returns all parts, laid end to end along the dimension named above; each array names one. Nothing has to cross between parts.
Inputs may be any that keep to these rules, and one draw needn't show every extreme that they name: Every value is positive; each diagonal block band[r, 0] is symmetric up to rounding. `far_tiles`: every value is positive. `far_list`: column 0 is a far block's row block, held by the device that stores the slot: device d along bin and blk holds row blocks 1 * d to 1 * d + 1 - 1. Column 1 is its column block, held by another device. Of the 16 slots of one device, used or not, exactly 4 have column blocks held by each of 4 other devices. The first far_count[d] slots of device d are used; some device uses all 16. `masked`: the entries of index g of bin are distinct bins of g * 512 to g * 512 + 511.
All inputs are finite; a program needn't handle non-finite values.
Results may differ from a plain program's by a relative error of at most 0.0001.
Values sent between devices are 32-bit elements; how exact they have to be, the bound alone decides.
A program may use at most 64 MiB of HBM per device.

v0:
```python
import jax
import jax.numpy as jnp
import numpy as np
from jax import lax
from jax.sharding import PartitionSpec as P

ITERS = 2


def band_tables(height, reach, depth):
    window = np.arange(height)[:, None] + np.arange(reach)[None, :]
    spread = np.zeros((height * reach, (depth + 1) * height), np.float32)
    for offset in range(1, reach):
        spread[offset, offset] = 1.0
    weight = np.full((reach,), 2.0, np.float32)
    weight[0] = 1.0
    return (window, jnp.asarray(spread), jnp.asarray(weight))


def local(band, far_tiles, far_list, far_count, masked):
    height = band.shape[0]
    reach = band.shape[1]
    block = band.shape[2]
    half = band.shape[3]
    slots = far_list.shape[0]
    owners = lax.axis_size(("bin", "blk"))
    device = lax.axis_index(("bin", "blk"))
    column_side = lax.axis_index("sub")
    depth = (reach + height - 2) // height
    window, spread, weight = band_tables(height, reach, depth)
    bin_index = device * (height * block) + lax.iota(jnp.int32, height * block)
    listed = jnp.any(bin_index[:, None] == masked[None, :], axis=1)
    keep = jnp.where(listed, 0.0, 1.0).astype(jnp.float32).reshape(height, block)
    valid_bins = owners * height * block - lax.axis_size("bin") * masked.shape[0]
    used = (lax.iota(jnp.int32, slots) < far_count[0]).astype(jnp.float32)
    far_rows = far_list[:, 0] - device * height
    far_cols = far_list[:, 1]
    row_pick = (far_rows[:, None] == lax.iota(jnp.int32, height)[None, :]).astype(jnp.float32)
    bias = keep
    coverage = keep
    for step in range(ITERS):
        own_half = lax.dynamic_slice_in_dim(bias, column_side * half, half, 1)
        gathered = lax.all_gather(own_half, ("bin", "blk"), axis=0, tiled=True)
        padded = jnp.concatenate([gathered, jnp.zeros((depth * height, half), jnp.float32)], axis=0)
        extended = lax.dynamic_slice_in_dim(padded, device * height, (depth + 1) * height, 0)
        remote_bias = gathered[far_cols]
        band_bias = extended[window]
        band_rows = jnp.einsum("atij,atj->ati", band, band_bias, precision=lax.Precision.HIGHEST)
        band_mirror = jnp.einsum("atij,ai->atj", band, bias, precision=lax.Precision.HIGHEST)
        far_own = jnp.dot(row_pick, bias, precision=lax.Precision.HIGHEST)
        far_forward = used[:, None] * jnp.einsum(
            "kij,kj->ki", far_tiles, remote_bias, precision=lax.Precision.HIGHEST
        )
        far_mirror = used[:, None] * jnp.einsum(
            "kij,ki->kj", far_tiles, far_own, precision=lax.Precision.HIGHEST
        )
        row_part = jnp.sum(band_rows, axis=1) + jnp.dot(
            row_pick.T, far_forward, precision=lax.Precision.HIGHEST
        )
        column_buffer = jnp.dot(
            spread.T, band_mirror.reshape(height * reach, half), precision=lax.Precision.HIGHEST
        )
        total_rows = owners * height
        placed = jnp.zeros((total_rows + depth * height, half), jnp.float32)
        placed = lax.dynamic_update_slice_in_dim(placed, column_buffer, device * height, 0)
        placed = placed[:total_rows].at[far_cols].add(far_mirror)
        column_half = lax.psum_scatter(placed, ("bin", "blk"), scatter_dimension=0, tiled=True)
        widened = lax.dynamic_update_slice_in_dim(
            jnp.zeros((height, block), jnp.float32), column_half, column_side * half, 1
        )
        sums = lax.psum(row_part + widened, "sub")
        coverage = bias * sums
        grand = lax.psum(jnp.sum(coverage), ("bin", "blk"))
        mean = grand / valid_bins
        bias = jnp.sqrt(bias * mean / sums)
    return (bias.reshape(-1), coverage.reshape(-1))


def solution(mesh):
    placed = (
        P(("grp", "bin", "blk"), None, None, "sub"),
        P(("grp", "bin", "blk"), None, "sub"),
        P(("grp", "bin", "blk"), None),
        P(("grp", "bin", "blk")),
        P(("grp", "bin")),
    )
    return jax.shard_map(
        local,
        mesh=mesh,
        in_specs=placed,
        out_specs=(P(("grp", "bin", "blk")), P(("grp", "bin", "blk"))),
        check_vma=False,
    )
```

profile of v0, /device:TPU:0, one launch (start us, length us, event | category | flops | bytes accessed | tf_op | source)
XLA Modules:
  0.0 141.0 jit_solution(9664757959378798546)
XLA Ops:
  0.7 0.9 compare_reduce_fusion
  1.7 22.1 %all-gather.1 = f32[8,1,128]{2,1,0:T(1,128)S(1)} all-gather(f32[1,1,128]{2,1,0:T(1,128)S(1)} %dynamic-slice_bitcast_fusion), channel_id=2, replica_groups=mesh['grp'=2,'bin'=4,'blk'=2,'sub'=2] {'bin','blk'}, dimensions={0}, use_global_device_ids=true | all-gather | bytes 4608 | tf_op jit(solution)/shard_map/all_gather | solution.py:43
  23.8 0.6 gather_fusion
  24.4 2.1 %fusion.6 = f32[1,256,1]{1,0,2:T(1,128)S(1)} fusion(f32[8,128,1]{1,2,0:T(1,128)S(1)} %bitcast.96, f32[1,8,256,128]{3,2,1,0:T(8,128)} %param.9), kind=kOutput, calls=%fused_computation.12 | convolution fusion | flops 3145728 | bytes 1053696 | tf_op jit(solution)/shard_map/atij,atj->ati/dot_general | solution.py:48
  26.5 0.7 fusion.30
  27.2 0.6 gather_fusion.1
  27.8 1.8 %fusion.34 = f32[16,1,256]{2,1,0:T(1,128)S(1)} fusion(f32[16,128,1]{1,2,0:T(1,128)S(1)} %bitcast.90, f32[16,256,128]{2,1,0:T(8,128)S(1)} %copy-done), kind=kOutput, calls=%fused_computation.64 | convolution fusion | flops 6291456 | bytes 2121728 | tf_op jit(solution)/shard_map/kij,kj->ki/dot_general | solution.py:51
  30.6 0.6 fusion.4
  31.6 1.1 fusion.13
  32.7 0.7 scatter_custom_fusion
  33.4 17.1 %all-reduce.2 = f32[8,128]{1,0:T(8,128)S(1)} all-reduce(f32[8,128]{1,0:T(8,128)S(1)} %scatter_custom_fusion), channel_id=3, replica_groups=mesh['grp'=2,'bin'=4,'blk'=2,'sub'=2] {'bin','blk'}, use_global_device_ids=true, to_apply=%region_2.3.clone | all-reduce | flops 1024 | bytes 8192
  50.6 0.6 dynamic-slice.14
  51.2 0.7 constant_dynamic-update-slice_fusion.1
  51.9 2.4 %psum.28 = f32[1,256]{1,0:T(1,128)S(1)} all-reduce(f32[1,256]{1,0:T(1,128)S(1)} %constant_dynamic-update-slice_fusion.1), channel_id=1, replica_groups=mesh['grp'=2,'bin'=4,'blk'=2,'sub'=2] {'sub'}, use_global_device_ids=true, to_apply=%region_3.4 | all-reduce | flops 256 | bytes 2048 | tf_op jit(solution)/shard_map/psum | solution.py:71
  54.3 0.6 multiply_reduce_fusion
  54.9 19.7 %psum.29 = f32[]{:T(128)} all-reduce(f32[]{:T(128)} %multiply_reduce_fusion), channel_id=1, replica_groups=mesh['grp'=2,'bin'=4,'blk'=2,'sub'=2] {'bin','blk'}, use_global_device_ids=true, to_apply=%region_5.6 | all-reduce | flops 1 | bytes 8 | tf_op jit(solution)/shard_map/psum | solution.py:73
  75.4 0.6 fusion
  76.0 0.2 fusion.37
  76.4 1.1 fusion.10
  77.5 0.7 scatter_custom_fusion.1
  78.2 17.1 %all-reduce.3 = f32[8,128]{1,0:T(8,128)S(1)} all-reduce(f32[8,128]{1,0:T(8,128)S(1)} %scatter_custom_fusion.1), channel_id=4, replica_groups=mesh['grp'=2,'bin'=4,'blk'=2,'sub'=2] {'bin','blk'}, use_global_device_ids=true, to_apply=%region_7.8.clone | all-reduce | flops 1024 | bytes 8192
  95.4 18.2 %all-gather.2 = f32[8,1,128]{2,1,0:T(1,128)S(1)} all-gather(f32[1,1,128]{2,1,0:T(1,128)S(1)} %fusion.29), channel_id=1, replica_groups=mesh['grp'=2,'bin'=4,'blk'=2,'sub'=2] {'bin','blk'}, dimensions={0}, use_global_device_ids=true | all-gather | bytes 4608 | tf_op jit(solution)/shard_map/all_gather | solution.py:43
  113.5 0.6 gather_fusion.3
  114.1 1.8 %fusion.36 = f32[16,1,256]{2,1,0:T(1,128)S(1)} fusion(f32[16,128,1]{1,2,0:T(1,128)S(1)} %bitcast.91, f32[16,256,128]{2,1,0:T(8,128)S(1)} %copy-done), kind=kOutput, calls=%fused_computation.66 | convolution fusion | flops 6291456 | bytes 2121728 | tf_op jit(solution)/shard_map/kij,kj->ki/dot_general | solution.py:51
  115.9 0.2 fusion.8
  116.1 0.6 gather_fusion.2
  116.7 0.9 fusion.2
  117.6 0.7 constant_dynamic-update-slice_fusion
  118.4 2.4 %psum.30 = f32[1,256]{1,0:T(1,128)S(1)} all-reduce(f32[1,256]{1,0:T(1,128)S(1)} %constant_dynamic-update-slice_fusion), channel_id=1, replica_groups=mesh['grp'=2,'bin'=4,'blk'=2,'sub'=2] {'sub'}, use_global_device_ids=true, to_apply=%region_8.9 | all-reduce | flops 256 | bytes 2048 | tf_op jit(solution)/shard_map/psum | solution.py:71
  120.8 1.2 fusion.31
  122.0 17.8 %psum.31 = f32[]{:T(128)} all-reduce(f32[]{:T(128)} %get-tuple-element.2), channel_id=1, replica_groups=mesh['grp'=2,'bin'=4,'blk'=2,'sub'=2] {'bin','blk'}, use_global_device_ids=true, to_apply=%region_10.11 | all-reduce | flops 1 | bytes 8 | tf_op jit(solution)/shard_map/psum | solution.py:73
  140.4 0.6 fusion.26
  (36 shorter events, 1.0 us)
Async XLA Ops:
  0.6 27.2 %copy-start = (f32[16,256,128]{2,1,0:T(8,128)S(1)}, f32[16,256,128]{2,1,0:T(8,128)}, u32[]{:S(2)}) copy-start(f32[16,256,128]{2,1,0:T(8,128)} %param.10) | copy-start | bytes 6291460
  0.6 29.9 %copy-start.1 = (f32[1,8,256,128]{3,2,1,0:T(8,128)S(1)}, f32[1,8,256,128]{3,2,1,0:T(8,128)}, u32[]{:S(2)}) copy-start(f32[1,8,256,128]{3,2,1,0:T(8,128)} %param.9) | copy-start | bytes 3145732
  0.7 29.7 %copy-start.3 = (s32[16,2]{0,1:T(2,128)S(1)}, s32[16,2]{0,1:T(2,128)}, u32[]{:S(2)}) copy-start(s32[16,2]{0,1:T(2,128)} %param.11) | copy-start | bytes 388
  24.4 6.8 %copy-start.2 = (f32[8,8]{1,0:T(8,128)S(1)}, f32[8,8]{1,0:T(8,128)}, u32[]{:S(2)}) copy-start(f32[8,8]{1,0:T(8,128)} %constant.45.clone) | copy-start | bytes 772
  29.6 20.9 %copy-start.4 = (u32[32]{0:T(128)S(1)}, u32[32]{0:T(128)}, u32[]{:S(2)}) copy-start(u32[32]{0:T(128)} %constant.59) | copy-start | bytes 388
where the time goes:
time: 141 us
  blocking collectives  117 us (83%)
  matrix products  10.9 us (8%)
  other arithmetic  7.06 us (5%)
  local copies, waits for them, and re-layouts  3.21 us (2%)
  between operations  2.83 us (2%)
    all_gather x2, blocking collectives, local(): gathered = lax.all_gather(own_half, ('bin', 'blk'), axis=0, tiled=True)  40.3 us
    psum x2, blocking collectives, local(): grand = lax.psum(jnp.sum(coverage), ('bin', 'blk'))  37.5 us
    unnamed x2, blocking collectives  34.3 us
    psum x2, blocking collectives, local(): sums = lax.psum(row_part + widened, 'sub')  4.89 us
    dot_general x2, matrix products, local(): jnp.einsum('kij,kj->ki', far_tiles, remote_bias, precision=lax.Precision....  3.66 us
    dot_general x2, matrix products, local(): jnp.einsum('atij,atj->ati', band, band_bias, precision=lax.Precision.HIGH...  3.06 us

commit v1 on v0

v1 whole, which is shorter than its diff:
```python
import functools

import jax
import jax.numpy as jnp
from jax import lax
from jax.experimental import pallas as pl
from jax.experimental.pallas import tpu as pltpu
from jax.sharding import PartitionSpec as P

MESH = pl.DeviceIdType.MESH
LANES = 128
GROUP = 32


def each(count, body):
    if count <= 16:
        for index in range(count):
            body(index)
    else:
        lax.fori_loop(0, count, lambda index, carry: (body(index), carry)[1], 0)


def landed(window, sem):
    pltpu.make_async_copy(window, window, sem).wait()


def to_column(row):
    parts = []
    for start in range(0, row.shape[1], LANES):
        piece = jnp.broadcast_to(row[:, start:start + LANES], (LANES, LANES))
        parts.append(jnp.transpose(piece))
    return jnp.concatenate(parts, axis=0)


def kernel(owners, blks, reach, slots, valid, masked, far_list, far_count, band, far_tiles,
           bias_out, cov_out, tiles, column, rows, bias_send, bias_first, bias_second, mirror_send, mirror_all,
           half_send, half_recv, total_send, total_all, load_sem, bias_sem, mirror_sem,
           half_sem, total_sem):
    bias_all = (bias_first, bias_second)
    height = column.shape[0]
    count = reach + slots
    device = lax.axis_index("bin") * blks + lax.axis_index("blk")
    side = lax.axis_index("sub")

    def place(owner, core):
        return {"bin": owner // blks, "blk": lax.rem(owner, blks), "sub": core}

    def other(index):
        return lax.rem(device + 1 + index, owners)

    loads = [pltpu.make_async_copy(band.at[0], tiles.at[pl.ds(0, reach)], load_sem.at[0])]
    half_slots = slots // 2
    for piece in range(2):
        loads.append(pltpu.make_async_copy(
            far_tiles.at[pl.ds(piece * half_slots, half_slots)],
            tiles.at[pl.ds(reach + piece * half_slots, half_slots)],
            load_sem.at[1 + piece],
        ))
    for load in loads:
        load.start()
    chunks = [(0, reach), (reach, reach + half_slots), (reach + half_slots, count)]

    barrier = pltpu.get_barrier_semaphore()

    def greet(index):
        pl.semaphore_signal(barrier, inc=1, device_id=place(other(index), side), device_id_type=MESH)

    def greet_across(index):
        pl.semaphore_signal(barrier, inc=1, device_id=place(index, 1 - side), device_id_type=MESH)

    each(owners - 1, greet)
    each(owners, greet_across)

    bins = device * height + lax.broadcasted_iota(jnp.int32, (1, height), 1)
    hit = bins == masked[0]
    for index in range(1, masked.shape[0]):
        hit = jnp.logical_or(hit, bins == masked[index])
    keep = jnp.where(hit, 0.0, 1.0).astype(jnp.float32)

    def own_half(row):
        return jnp.where(side == 0, row[:, :LANES], row[:, LANES:])

    for step in range(2):
        bias_all[step][pl.ds(owners, reach), :] = jnp.zeros((reach, LANES), jnp.float32)
        mirror_all[step, pl.ds(device, 1), :] = jnp.zeros((1, LANES), jnp.float32)

    def send_bias(step, row):
        half = own_half(row)
        bias_send[step] = half
        bias_all[step][pl.ds(device, 1), :] = half

        def send(index):
            pltpu.make_async_remote_copy(
                src_ref=bias_send.at[step],
                dst_ref=bias_all[step].at[pl.ds(device, 1)],
                send_sem=bias_sem.at[0, step],
                recv_sem=bias_sem.at[1, step],
                device_id=place(other(index), side),
                device_id_type=MESH,
            ).start()

        each(owners - 1, send)

    used = [index < far_count[0] for index in range(slots)]

    def mirror(step, wait):
        sums = []
        for number, (first, last) in enumerate(chunks):
            if wait:
                loads[number].wait()
            first_tile = max(first, 1)

            def body(index, held):
                window = pl.ds(pl.multiple_of(index * GROUP, GROUP), GROUP)
                own = column[window, :]
                return tuple(
                    old + jnp.sum((tiles[first_tile + at, window, :] * own).reshape(GROUP // 8, 8, LANES), axis=0)
                    for at, old in enumerate(held)
                )

            zero = jnp.zeros((8, LANES), jnp.float32)
            sums.extend(lax.fori_loop(0, height // GROUP, body, (zero,) * (last - first_tile)))
        holder = lax.broadcasted_iota(jnp.int32, (owners, LANES), 0)
        placed = jnp.zeros((owners, LANES), jnp.float32)
        for at, partial in enumerate(sums):
            tile = at + 1
            if tile < reach:
                target = device + tile
            else:
                slot = tile - reach
                target = jnp.where(used[slot], far_list[slot, 1], -1)
            total = jnp.sum(partial, axis=0, keepdims=True)
            placed = placed + jnp.where(holder == target, total, 0.0)
        mirror_send[step] = placed

    def send_mirror(step):
        def send(index):
            owner = other(index)
            pltpu.make_async_remote_copy(
                src_ref=mirror_send.at[step, pl.ds(owner, 1)],
                dst_ref=mirror_all.at[step, pl.ds(device, 1)],
                send_sem=mirror_sem.at[0, step],
                recv_sem=mirror_sem.at[1, step],
                device_id=place(owner, side),
                device_id_type=MESH,
            ).start()

        each(owners - 1, send)

    def forward(step):
        landed(bias_all[step].at[pl.ds(0, owners - 1)], bias_sem.at[1, step])
        factors = []
        for tile in range(count):
            if tile < reach:
                factor = bias_all[step][pl.ds(device + tile, 1), :]
            else:
                slot = tile - reach
                factor = bias_all[step][pl.ds(far_list[slot, 1], 1), :]
                factor = jnp.where(used[slot], factor, 0.0)
            factors.append(jnp.broadcast_to(factor, (8, LANES))[None])

        def body(index, form):
            window = pl.ds(pl.multiple_of(index * GROUP, GROUP), GROUP)

            def term(tile):
                return tiles[tile, window, :].reshape(GROUP // 8, 8, LANES) * factors[tile]

            near = term(0)
            far = term(1)
            for tile in range(2, count):
                far = far + term(tile)
            whole = near + far
            rows[window, :] = whole.reshape(GROUP, LANES)
            if step == 0:
                return form
            own = column[window, :].reshape(GROUP // 8, 8, LANES)
            return form + jnp.sum(own * (whole + far), axis=0)

        form = lax.fori_loop(0, height // GROUP, body, jnp.zeros((8, LANES), jnp.float32))
        pieces = []
        for start in range(0, height, LANES):
            piece = jnp.transpose(rows[pl.ds(start, LANES), :])
            pieces.append(jnp.sum(piece, axis=0, keepdims=True))
        return jnp.concatenate(pieces, axis=1), jnp.sum(form, axis=0, keepdims=True)

    def join(step, row_part):
        landed(mirror_all.at[step, pl.ds(0, owners - 1)], mirror_sem.at[1, step])
        col_half = jnp.sum(mirror_all[step], axis=0, keepdims=True)
        empty = jnp.zeros_like(col_half)
        part = row_part + jnp.concatenate(
            [jnp.where(side == 0, col_half, empty), jnp.where(side == 0, empty, col_half)], axis=1
        )
        half_send[step] = part
        copy = pltpu.make_async_remote_copy(
            src_ref=half_send.at[step],
            dst_ref=half_recv.at[step],
            send_sem=half_sem.at[0, step],
            recv_sem=half_sem.at[1, step],
            device_id=place(device, 1 - side),
            device_id_type=MESH,
        )
        copy.start()
        copy.wait_recv()
        return part + half_recv[step]

    column[...] = to_column(keep)
    pl.semaphore_wait(barrier, 2 * owners - 1)
    send_bias(0, keep)
    mirror(0, True)
    send_mirror(0)
    row_part, _ = forward(0)
    sums = join(0, row_part)

    scaled = keep / jnp.sqrt(sums)
    send_bias(1, scaled)
    column[...] = to_column(scaled)
    mirror(1, False)
    send_mirror(1)
    row_part, form = forward(1)

    packet = jnp.concatenate([own_half(keep * sums), form], axis=0)
    total_send[...] = packet
    total_all[device * 2 + side] = packet

    def send_total(owner, core):
        pltpu.make_async_remote_copy(
            src_ref=total_send,
            dst_ref=total_all.at[device * 2 + side],
            send_sem=total_sem.at[0],
            recv_sem=total_sem.at[1],
            device_id=place(owner, core),
            device_id_type=MESH,
        ).start()

    each(owners - 1, lambda index: send_total(other(index), side))
    each(owners, lambda index: send_total(index, 1 - side))
    product = join(1, row_part)
    landed(total_all.at[pl.ds(0, 2 * owners - 1)], total_sem.at[1])
    totals = jnp.sum(jnp.sum(total_all[...], axis=0), axis=1, keepdims=True) / valid
    first = totals[0:1]
    mean = first * totals[1:2]
    bias_out[...] = jnp.sqrt(scaled * mean / product)
    cov_out[...] = scaled * product * first

    for step in range(2):
        landed(bias_all[step].at[pl.ds(0, owners - 1)], bias_sem.at[0, step])
        landed(mirror_all.at[step, pl.ds(0, owners - 1)], mirror_sem.at[0, step])
        landed(half_send.at[step], half_sem.at[0, step])
    landed(total_all.at[pl.ds(0, 2 * owners - 1)], total_sem.at[0])


def local(band, far_tiles, far_list, far_count, masked):
    reach, block, half = band.shape[1:]
    slots = far_tiles.shape[0]
    owners = lax.axis_size(("bin", "blk"))
    valid = owners * block - lax.axis_size("bin") * masked.shape[0]
    smem = pl.BlockSpec(memory_space=pltpu.SMEM)
    hbm = pl.BlockSpec(memory_space=pl.ANY)
    vmem = pl.BlockSpec(memory_space=pltpu.VMEM)
    f32 = jnp.float32
    dma = pltpu.SemaphoreType.DMA
    bias, coverage = pl.pallas_call(
        functools.partial(kernel, owners, lax.axis_size("blk"), reach, slots, float(valid)),
        out_shape=(jax.ShapeDtypeStruct((1, block), f32), jax.ShapeDtypeStruct((1, block), f32)),
        in_specs=[smem, smem, smem, hbm, hbm],
        out_specs=(vmem, vmem),
        scratch_shapes=[
            pltpu.VMEM((reach + slots, block, half), f32),
            pltpu.VMEM((block, half), f32),
            pltpu.VMEM((block, half), f32),
            pltpu.VMEM((2, 1, half), f32),
            pltpu.VMEM((owners + reach, half), f32),
            pltpu.VMEM((owners + reach, half), f32),
            pltpu.VMEM((2, owners, half), f32),
            pltpu.VMEM((2, owners, half), f32),
            pltpu.VMEM((2, 1, block), f32),
            pltpu.VMEM((2, 1, block), f32),
            pltpu.VMEM((2, half), f32),
            pltpu.VMEM((2 * owners, 2, half), f32),
            dma((3,)),
            dma((2, 2)),
            dma((2, 2)),
            dma((2, 2)),
            dma((2,)),
        ],
        compiler_params=pltpu.CompilerParams(collective_id=0, has_side_effects=True),
    )(masked, far_list, far_count, band, far_tiles)
    return bias.reshape(-1), coverage.reshape(-1)


def solution(mesh):
    placed = (
        P(("grp", "bin", "blk"), None, None, "sub"),
        P(("grp", "bin", "blk"), None, "sub"),
        P(("grp", "bin", "blk"), None),
        P(("grp", "bin", "blk")),
        P(("grp", "bin")),
    )
    return jax.shard_map(
        local,
        mesh=mesh,
        in_specs=placed,
        out_specs=(P(("grp", "bin", "blk")), P(("grp", "bin", "blk"))),
        check_vma=False,
    )
```

time: 141 us -> 24.8 us (0.18)
  blocking collectives: 117 us -> 0 us
  Pallas kernels: 0 us -> 19.5 us
  matrix products: 10.9 us -> 0 us
  other arithmetic: 7.06 us -> 0 us
  between operations: 2.83 us -> 1.29 us
    psum x4 -> x0, blocking collectives: 42.4 us -> none  [the longest x2 37.5 us: local(): grand = lax.psum(jnp.sum(coverage), ('bin', 'blk'))]
    all_gather x2 -> x0, blocking collectives: 40.3 us -> none  [local(): gathered = lax.all_gather(own_half, ('bin', 'blk'), axis=0, tiled=True)]
    unnamed x2 -> x0, blocking collectives: 34.3 us -> none
    pallas_call x0 -> x1, Pallas kernels: none -> 19.5 us  [local(): pl.pallas_call(functools.partial(kernel, owners, lax.axis_size('blk'), re...]
    dot_general x12 -> x0, matrix products: 10.9 us -> none  [the longest x2 3.66 us: local(): jnp.einsum('kij,kj->ki', far_tiles, remote_bias, precision=lax.Precision....]
    unnamed x15 -> x3, local copies, waits for them, and re-layouts: 0.72 us -> 3.79 us
    gather x4 -> x0, local copies, waits for them, and re-layouts: 2.23 us -> none  [the longest x2 1.12 us: local(): remote_bias = gathered[far_cols]]
    reduce_sum x2 -> x0, other arithmetic: 1.77 us -> none  [local(): grand = lax.psum(jnp.sum(coverage), ('bin', 'blk'))]
where the time goes in v1:
time: 24.8 us; the launch traced here: 24.5 us
  Pallas kernels  19.5 us (79%)
  local copies, waits for them, and re-layouts  3.79 us (15%)
  between operations  1.29 us (5%)
    pallas_call x1, Pallas kernels, local(): pl.pallas_call(functools.partial(kernel, owners, lax.axis_size('blk'), re...  19.5 us
    unnamed x3, local copies, waits for them, and re-layouts  3.79 us

profile of v1, /device:TPU:0, one launch (start us, length us, event | category | flops | bytes accessed | tf_op | source)
XLA Modules:
  0.0 24.5 jit_solution(13241841851988236412)
XLA Ops:
  1.3 1.3 %copy.7.far_list = s32[16,2]{1,0:T(8,128)} copy(s32[16,2]{0,1:T(2,128)} %param.7) | data formatting | bytes 256 | tf_op args[2]
  2.6 19.5 %shard_map.68 = (f32[1,256]{1,0:T(1,128)}, f32[1,256]{1,0:T(1,128)}) custom-call(s32[32]{0:T(128)} %masked.1, s32[16,2]{1,0:T(8,128)} %copy.7.far_list, s32[1]{0:T(128)S(6)} %copy.10.far_count, f32[1,8,256,128]{3,2,1,0:T(8,128)} %band.1, f32[16,256,128]{2,1,0:T(8,128)} %far_tiles.1), custom_call_target="tpu_custom_call" | custom-call | tf_op jit(solution)/shard_map/pallas_call | solution.py:262
  22.1 1.2 %copy.11 = f32[256]{0:T(256)} copy(f32[256]{0:T(256)} %bitcast.3) | data formatting | bytes 2048
  23.3 1.2 %copy.12 = f32[256]{0:T(256)} copy(f32[256]{0:T(256)} %bitcast.2) | data formatting | bytes 2048

commit v2 on v1

v2 whole, which is shorter than its diff:
```python
import functools

import jax
import jax.numpy as jnp
from jax import lax
from jax.experimental import pallas as pl
from jax.experimental.pallas import tpu as pltpu
from jax.sharding import PartitionSpec as P

MESH = pl.DeviceIdType.MESH
LANES = 128
GROUP = 32


def each(count, body):
    if count <= 16:
        for index in range(count):
            body(index)
    else:
        lax.fori_loop(0, count, lambda index, carry: (body(index), carry)[1], 0)


def landed(window, sem):
    pltpu.make_async_copy(window, window, sem).wait()


def to_column(row):
    parts = []
    for start in range(0, row.shape[1], LANES):
        piece = jnp.broadcast_to(row[:, start:start + LANES], (LANES, LANES))
        parts.append(jnp.transpose(piece))
    return jnp.concatenate(parts, axis=0)


def kernel(owners, blks, reach, slots, valid, masked_hbm, list_hbm, count_hbm, band, far_tiles,
           weight_out, product_out, level_out, masked, far_list, far_count, tiles, column, rows, products, keep_send, keep_all,
           scaled_all, mirror_send, mirror_all, same_send, same_all, cross_send, cross_all,
           pair_send, pair_recv, half_send, half_recv, total_send, total_all, word_sem, load_sem,
           keep_sem, mirror_sem, same_sem, cross_sem, pair_sem, half_sem, total_sem):
    height = column.shape[0]
    count = reach + slots
    device = lax.axis_index("bin") * blks + lax.axis_index("blk")
    side = lax.axis_index("sub")

    def place(owner, core):
        return {"bin": owner // blks, "blk": lax.rem(owner, blks), "sub": core}

    def other(index):
        return lax.rem(device + 1 + index, owners)

    barrier = pltpu.get_barrier_semaphore()

    def greet(index):
        for core in (side, 1 - side):
            pl.semaphore_signal(
                barrier, inc=1, device_id=place(other(index), core), device_id_type=MESH
            )

    each(owners - 1, greet)
    pl.semaphore_signal(barrier, inc=1, device_id=place(device, 1 - side), device_id_type=MESH)

    words = [
        pltpu.make_async_copy(source, target, word_sem.at[at])
        for at, (source, target) in enumerate(
            ((masked_hbm, masked), (list_hbm, far_list), (count_hbm, far_count))
        )
    ]
    for word in words:
        word.start()
    loads = [pltpu.make_async_copy(band.at[0], tiles.at[pl.ds(0, reach)], load_sem.at[0])]
    half_slots = slots // 2
    for piece in range(2):
        loads.append(pltpu.make_async_copy(
            far_tiles.at[pl.ds(piece * half_slots, half_slots)],
            tiles.at[pl.ds(reach + piece * half_slots, half_slots)],
            load_sem.at[1 + piece],
        ))
    for load in loads:
        load.start()
    chunks = [(0, reach), (reach, reach + half_slots), (reach + half_slots, count)]

    keep_all[pl.ds(owners, reach), :] = jnp.zeros((reach, LANES), jnp.float32)
    scaled_all[pl.ds(owners, reach), :] = jnp.zeros((reach, LANES), jnp.float32)
    for step in range(2):
        mirror_all[step, pl.ds(device, 1), :] = jnp.zeros((1, LANES), jnp.float32)

    for word in words:
        word.wait()
    bins = device * height + lax.broadcasted_iota(jnp.int32, (1, height), 1)
    hit = bins == masked[0]
    for index in range(1, masked.shape[0]):
        hit = jnp.logical_or(hit, bins == masked[index])
    keep = jnp.where(hit, 0.0, 1.0).astype(jnp.float32)
    used = [index < far_count[0] for index in range(slots)]

    def send(source, target, sem, owner, core):
        copy = pltpu.make_async_remote_copy(
            src_ref=source,
            dst_ref=target,
            send_sem=sem[0],
            recv_sem=sem[1],
            device_id=place(owner, core),
            device_id_type=MESH,
        )
        copy.start()
        return copy

    def pick(row, core):
        return jnp.where(core == 0, row[:, :LANES], row[:, LANES:])

    def merge(own, across):
        return jnp.concatenate(
            [jnp.where(side == 0, own, across), jnp.where(side == 0, across, own)], axis=1
        )

    mine = pl.ds(device, 1)

    def mirror(step):
        sums = []
        for number, (first, last) in enumerate(chunks):
            if step == 0:
                loads[number].wait()

            def body(index, held):
                window = pl.ds(pl.multiple_of(index * GROUP, GROUP), GROUP)
                own = column[window, :]
                return tuple(
                    old + jnp.sum((tiles[first + at, window, :] * own).reshape(GROUP // 8, 8, LANES), axis=0)
                    for at, old in enumerate(held)
                )

            zero = jnp.zeros((8, LANES), jnp.float32)
            sums.extend(lax.fori_loop(0, height // GROUP, body, (zero,) * (last - first)))
        holder = lax.broadcasted_iota(jnp.int32, (owners, LANES), 0)
        placed = jnp.zeros((owners, LANES), jnp.float32)
        for tile, partial in enumerate(sums):
            if step == 1:
                products[tile] = partial
            if tile == 0:
                continue
            if tile < reach:
                target = device + tile
            else:
                slot = tile - reach
                target = jnp.where(used[slot], far_list[1, slot], -1)
            total = jnp.sum(partial, axis=0, keepdims=True)
            placed = placed + jnp.where(holder == target, total, 0.0)
        mirror_send[step] = placed

        def push(index):
            owner = other(index)
            send(mirror_send.at[step, pl.ds(owner, 1)], mirror_all.at[step, mine],
                 (mirror_sem.at[0, step], mirror_sem.at[1, step]), owner, side)

        each(owners - 1, push)

    def gather(source):
        factors = []
        for tile in range(count):
            if tile < reach:
                factor = source[pl.ds(device + tile, 1), :]
            else:
                slot = tile - reach
                factor = jnp.where(used[slot], source[pl.ds(far_list[1, slot], 1), :], 0.0)
            factors.append(jnp.broadcast_to(factor, (8, LANES)))
        return factors

    def forward(factors):
        def body(index, carry):
            window = pl.ds(pl.multiple_of(index * GROUP, GROUP), GROUP)

            def term(tile):
                return tiles[tile, window, :].reshape(GROUP // 8, 8, LANES) * factors[tile][None]

            whole = term(0)
            for tile in range(1, count):
                whole = whole + term(tile)
            rows[window, :] = whole.reshape(GROUP, LANES)
            return carry

        lax.fori_loop(0, height // GROUP, body, 0)
        pieces = []
        for start in range(0, height, LANES):
            piece = jnp.transpose(rows[pl.ds(start, LANES), :])
            pieces.append(jnp.sum(piece, axis=0, keepdims=True))
        return jnp.concatenate(pieces, axis=1)

    def mirrored(step):
        landed(mirror_all.at[step, pl.ds(0, owners - 1)], mirror_sem.at[1, step])
        return jnp.sum(mirror_all[step], axis=0, keepdims=True)

    keep_half = pick(keep, side)
    keep_send[...] = keep_half
    keep_all[mine, :] = keep_half
    column[...] = to_column(keep)
    pl.semaphore_wait(barrier, 2 * owners - 1)
    each(owners - 1, lambda index: send(
        keep_send, keep_all.at[mine], (keep_sem.at[0], keep_sem.at[1]), other(index), side))
    mirror(0)
    landed(keep_all.at[pl.ds(0, owners - 1)], keep_sem.at[1])
    row_part = forward(gather(keep_all))
    same = pick(row_part, side) + mirrored(0)
    cross = pick(row_part, 1 - side)
    same_send[...] = same
    same_all[mine, :] = same
    cross_send[...] = cross
    pair_send[...] = jnp.concatenate([cross, same], axis=0)

    def spread(index):
        owner = other(index)
        send(same_send, same_all.at[mine], (same_sem.at[0], same_sem.at[1]), owner, side)
        send(cross_send, cross_all.at[mine], (cross_sem.at[0], cross_sem.at[1]), owner, 1 - side)

    each(owners - 1, spread)
    pair = send(pair_send, pair_recv, (pair_sem.at[0], pair_sem.at[1]), device, 1 - side)
    pair.wait_recv()
    across = pair_recv[0:1, :]
    cross_all[mine, :] = across
    sums = merge(same + across, cross + pair_recv[1:2, :])
    scaled = keep / jnp.sqrt(sums)
    column[...] = to_column(scaled)
    mirror(1)
    landed(same_all.at[pl.ds(0, owners - 1)], same_sem.at[1])
    landed(cross_all.at[pl.ds(0, owners - 1)], cross_sem.at[1])
    scaled_all[pl.ds(0, owners), :] = keep_all[pl.ds(0, owners), :] / jnp.sqrt(same_all[...] + cross_all[...])
    factors = gather(scaled_all)
    form = products[1] * factors[1]
    for tile in range(2, count):
        form = form + products[tile] * factors[tile]
    form = jnp.sum(products[0] * factors[0] + 2.0 * form, axis=0, keepdims=True)
    packet = jnp.concatenate([pick(keep * sums, side), form], axis=0)
    total_send[...] = packet
    slot = device * 2 + side
    total_all[slot] = packet
    pair_total = (total_sem.at[0], total_sem.at[1])

    def announce(index):
        for core in (side, 1 - side):
            send(total_send, total_all.at[slot], pair_total, other(index), core)

    each(owners - 1, announce)
    send(total_send, total_all.at[slot], pair_total, device, 1 - side)

    row_part = forward(factors)
    col_half = mirrored(1)
    part = row_part + merge(col_half, jnp.zeros_like(col_half))
    half_send[...] = part
    half = send(half_send, half_recv, (half_sem.at[0], half_sem.at[1]), device, 1 - side)
    half.wait_recv()
    product = part + half_recv[...]
    landed(total_all.at[pl.ds(0, 2 * owners - 1)], total_sem.at[1])
    totals = jnp.sum(jnp.sum(total_all[...], axis=0), axis=1, keepdims=True) / valid
    first = totals[0:1]
    mean = first * totals[1:2]
    weight_out[...] = scaled * first
    product_out[...] = product
    level_out[...] = scaled * mean

    landed(keep_all.at[pl.ds(0, owners - 1)], keep_sem.at[0])
    landed(same_all.at[pl.ds(0, owners - 1)], same_sem.at[0])
    landed(cross_all.at[pl.ds(0, owners - 1)], cross_sem.at[0])
    pair.wait_send()
    half.wait_send()
    for step in range(2):
        landed(mirror_all.at[step, pl.ds(0, owners - 1)], mirror_sem.at[0, step])
    landed(total_all.at[pl.ds(0, 2 * owners - 1)], total_sem.at[0])


def local(band, far_tiles, far_list, far_count, masked):
    reach, block, half = band.shape[1:]
    slots = far_tiles.shape[0]
    owners = lax.axis_size(("bin", "blk"))
    valid = owners * block - lax.axis_size("bin") * masked.shape[0]
    hbm = pl.BlockSpec(memory_space=pl.ANY)
    vmem = pl.BlockSpec(memory_space=pltpu.VMEM)
    f32 = jnp.float32
    dma = pltpu.SemaphoreType.DMA
    weight, product, level = pl.pallas_call(
        functools.partial(kernel, owners, lax.axis_size("blk"), reach, slots, float(valid)),
        out_shape=(jax.ShapeDtypeStruct((1, block), f32),) * 3,
        out_specs=(vmem,) * 3,
        in_specs=[hbm] * 5,
        scratch_shapes=[
            pltpu.SMEM(masked.shape, jnp.int32),
            pltpu.SMEM((2, slots), jnp.int32),
            pltpu.SMEM((1,), jnp.int32),
            pltpu.VMEM((reach + slots, block, half), f32),
            pltpu.VMEM((block, half), f32),
            pltpu.VMEM((block, half), f32),
            pltpu.VMEM((reach + slots, 8, half), f32),
            pltpu.VMEM((1, half), f32),
            pltpu.VMEM((owners + reach, half), f32),
            pltpu.VMEM((owners + reach, half), f32),
            pltpu.VMEM((2, owners, half), f32),
            pltpu.VMEM((2, owners, half), f32),
            pltpu.VMEM((1, half), f32),
            pltpu.VMEM((owners, half), f32),
            pltpu.VMEM((1, half), f32),
            pltpu.VMEM((owners, half), f32),
            pltpu.VMEM((2, half), f32),
            pltpu.VMEM((2, half), f32),
            pltpu.VMEM((1, block), f32),
            pltpu.VMEM((1, block), f32),
            pltpu.VMEM((2, half), f32),
            pltpu.VMEM((2 * owners, 2, half), f32),
            dma((3,)),
            dma((3,)),
            dma((2,)),
            dma((2, 2)),
            dma((2,)),
            dma((2,)),
            dma((2,)),
            dma((2,)),
            dma((2,)),
        ],
        compiler_params=pltpu.CompilerParams(collective_id=0, has_side_effects=True),
    )(masked, far_list.T, far_count, band, far_tiles)
    weight, product, level = weight.reshape(-1), product.reshape(-1), level.reshape(-1)
    return jnp.sqrt(level / product), weight * product


def solution(mesh):
    placed = (
        P(("grp", "bin", "blk"), None, None, "sub"),
        P(("grp", "bin", "blk"), None, "sub"),
        P(("grp", "bin", "blk"), None),
        P(("grp", "bin", "blk")),
        P(("grp", "bin")),
    )
    return jax.shard_map(
        local,
        mesh=mesh,
        in_specs=placed,
        out_specs=(P(("grp", "bin", "blk")), P(("grp", "bin", "blk"))),
        check_vma=False,
    )
```

time: 24.8 us -> 21.3 us (0.86)
  local copies, waits for them, and re-layouts: 3.79 us -> 0 us
  other arithmetic: 0 us -> 1.25 us
  Pallas kernels: 19.5 us -> 18.6 us
    unnamed x3 -> x0, local copies, waits for them, and re-layouts: 3.79 us -> none
    mul x0 -> x1, other arithmetic: none -> 1.25 us  [local(): return (jnp.sqrt(level / product), weight * product)]
    pallas_call x1, Pallas kernels: 19.5 us -> 18.6 us  [local(): pl.pallas_call(functools.partial(kernel, owners, lax.axis_size('blk'), re...]
where the time goes in v2:
time: 21.3 us; the launch traced here: 21.1 us
  Pallas kernels  18.6 us (87%)
  between operations  1.29 us (6%)
  other arithmetic  1.25 us (6%)
    pallas_call x1, Pallas kernels, local(): pl.pallas_call(functools.partial(kernel, owners, lax.axis_size('blk'), re...  18.6 us
    mul x1, other arithmetic, local(): return (jnp.sqrt(level / product), weight * product)  1.25 us

profile of v2, /device:TPU:0, one launch (start us, length us, event | category | flops | bytes accessed | tf_op | source)
XLA Modules:
  0.0 21.1 jit_solution(3242028902560400387)
XLA Ops:
  1.3 18.6 %shard_map.68 = (f32[1,256]{1,0:T(1,128)}, f32[1,256]{1,0:T(1,128)}, f32[1,256]{1,0:T(1,128)}) custom-call(s32[32]{0:T(128)} %masked_hbm.1, s32[2,16]{1,0:T(2,128)} %bitcast.3, s32[1]{0:T(128)S(6)} %copy.7.count_hbm, f32[1,8,256,128]{3,2,1,0:T(8,128)} %band.1, f32[16,256,128]{2,1,0:T(8,128)} %far_tiles.1), custom_call_target="tpu_custom_call" | custom-call | tf_op jit(solution)/shard_map/pallas_call | solution.py:278
  19.9 1.2 %fusion = (f32[1,256]{1,0:T(1,128)}, f32[1,256]{1,0:T(1,128)}) fusion(f32[1,256]{1,0:T(1,128)} %get-tuple-element.7, f32[1,256]{1,0:T(1,128)} %get-tuple-element.6, f32[1,256]{1,0:T(1,128)} %get-tuple-element.5), kind=kLoop, calls=%fused_computation.1 | loop fusion | flops 512 | bytes 5120 | tf_op jit(solution)/shard_map/mul | solution.py:319

commit v3 on v2

--- a/solution.py
+++ b/solution.py
@@ -9,6 +9,7 @@
 
 MESH = pl.DeviceIdType.MESH
 LANES = 128
+PIECE = 2
 GROUP = 32
 
 
@@ -56,8 +57,6 @@
                 barrier, inc=1, device_id=place(other(index), core), device_id_type=MESH
             )
 
-    each(owners - 1, greet)
-    pl.semaphore_signal(barrier, inc=1, device_id=place(device, 1 - side), device_id_type=MESH)
 
     words = [
         pltpu.make_async_copy(source, target, word_sem.at[at])
@@ -67,17 +66,18 @@
     ]
     for word in words:
         word.start()
-    loads = [pltpu.make_async_copy(band.at[0], tiles.at[pl.ds(0, reach)], load_sem.at[0])]
     half_slots = slots // 2
-    for piece in range(2):
-        loads.append(pltpu.make_async_copy(
-            far_tiles.at[pl.ds(piece * half_slots, half_slots)],
-            tiles.at[pl.ds(reach + piece * half_slots, half_slots)],
-            load_sem.at[1 + piece],
-        ))
-    for load in loads:
-        load.start()
     chunks = [(0, reach), (reach, reach + half_slots), (reach + half_slots, count)]
+    for number, (first, last) in enumerate(chunks):
+        source = band.at[0] if number == 0 else far_tiles
+        skip = 0 if number == 0 else reach
+        for at in range(first, last, PIECE):
+            pltpu.make_async_copy(
+                source.at[pl.ds(at - skip, PIECE)], tiles.at[pl.ds(at, PIECE)], load_sem.at[number]
+            ).start()
+
+    each(owners - 1, greet)
+    pl.semaphore_signal(barrier, inc=1, device_id=place(device, 1 - side), device_id_type=MESH)
 
     keep_all[pl.ds(owners, reach), :] = jnp.zeros((reach, LANES), jnp.float32)
     scaled_all[pl.ds(owners, reach), :] = jnp.zeros((reach, LANES), jnp.float32)
@@ -119,7 +119,7 @@
         sums = []
         for number, (first, last) in enumerate(chunks):
             if step == 0:
-                loads[number].wait()
+                landed(tiles.at[pl.ds(first, last - first)], load_sem.at[number])
 
             def body(index, held):
                 window = pl.ds(pl.multiple_of(index * GROUP, GROUP), GROUP)
@@ -166,21 +166,18 @@
         return factors
 
     def forward(factors):
-        def body(index, carry):
-            window = pl.ds(pl.multiple_of(index * GROUP, GROUP), GROUP)
-
-            def term(tile):
-                return tiles[tile, window, :].reshape(GROUP // 8, 8, LANES) * factors[tile][None]
-
-            whole = term(0)
-            for tile in range(1, count):
-                whole = whole + term(tile)
-            rows[window, :] = whole.reshape(GROUP, LANES)
-            return carry
-
-        lax.fori_loop(0, height // GROUP, body, 0)
         pieces = []
         for start in range(0, height, LANES):
+            for at in range(start, start + LANES, GROUP):
+                window = pl.ds(at, GROUP)
+
+                def term(tile):
+                    return tiles[tile, window, :].reshape(GROUP // 8, 8, LANES) * factors[tile][None]
+
+                whole = term(0)
+                for tile in range(1, count):
+                    whole = whole + term(tile)
+                rows[window, :] = whole.reshape(GROUP, LANES)
             piece = jnp.transpose(rows[pl.ds(start, LANES), :])
             pieces.append(jnp.sum(piece, axis=0, keepdims=True))
         return jnp.concatenate(pieces, axis=1)

time: 21.3 us -> 21 us (0.986)
  Pallas kernels: 18.6 us -> 18.3 us
    pallas_call x1, Pallas kernels: 18.6 us -> 18.3 us  [local(): pl.pallas_call(functools.partial(kernel, owners, lax.axis_size('blk'), re...]
where the time goes in v3:
time: 21 us; the launch traced here: 20.9 us
  Pallas kernels  18.3 us (87%)
  between operations  1.29 us (6%)
  other arithmetic  1.25 us (6%)
    pallas_call x1, Pallas kernels, local(): pl.pallas_call(functools.partial(kernel, owners, lax.axis_size('blk'), re...  18.3 us
    mul x1, other arithmetic, local(): return (jnp.sqrt(level / product), weight * product)  1.25 us

profile of v3, /device:TPU:0, one launch (start us, length us, event | category | flops | bytes accessed | tf_op | source)
XLA Modules:
  0.0 20.9 jit_solution(16465578692828145386)
XLA Ops:
  1.3 18.3 %shard_map.68 = (f32[1,256]{1,0:T(1,128)}, f32[1,256]{1,0:T(1,128)}, f32[1,256]{1,0:T(1,128)}) custom-call(s32[32]{0:T(128)} %masked_hbm.1, s32[2,16]{1,0:T(2,128)} %bitcast.3, s32[1]{0:T(128)S(6)} %copy.7.count_hbm, f32[1,8,256,128]{3,2,1,0:T(8,128)} %band.1, f32[16,256,128]{2,1,0:T(8,128)} %far_tiles.1), custom_call_target="tpu_custom_call" | custom-call | tf_op jit(solution)/shard_map/pallas_call | solution.py:275
  19.6 1.2 %fusion = (f32[1,256]{1,0:T(1,128)}, f32[1,256]{1,0:T(1,128)}) fusion(f32[1,256]{1,0:T(1,128)} %get-tuple-element.7, f32[1,256]{1,0:T(1,128)} %get-tuple-element.6, f32[1,256]{1,0:T(1,128)} %get-tuple-element.5), kind=kLoop, calls=%fused_computation.1 | loop fusion | flops 512 | bytes 5120 | tf_op jit(solution)/shard_map/mul | solution.py:316

commit v4 on v3

--- a/solution.py
+++ b/solution.py
@@ -33,8 +33,8 @@
     return jnp.concatenate(parts, axis=0)
 
 
-def kernel(owners, blks, reach, slots, valid, masked_hbm, list_hbm, count_hbm, band, far_tiles,
-           weight_out, product_out, level_out, masked, far_list, far_count, tiles, column, rows, products, keep_send, keep_all,
+def kernel(owners, blks, reach, slots, valid, masked_hbm, list_hbm, far_count, band, far_tiles,
+           weight_out, product_out, level_out, masked, far_list, tiles, column, rows, products, keep_send, keep_all,
            scaled_all, mirror_send, mirror_all, same_send, same_all, cross_send, cross_all,
            pair_send, pair_recv, half_send, half_recv, total_send, total_all, word_sem, load_sem,
            keep_sem, mirror_sem, same_sem, cross_sem, pair_sem, half_sem, total_sem):
@@ -61,7 +61,7 @@
     words = [
         pltpu.make_async_copy(source, target, word_sem.at[at])
         for at, (source, target) in enumerate(
-            ((masked_hbm, masked), (list_hbm, far_list), (count_hbm, far_count))
+            ((masked_hbm, masked), (list_hbm, far_list))
         )
     ]
     for word in words:
@@ -214,12 +214,12 @@
     across = pair_recv[0:1, :]
     cross_all[mine, :] = across
     sums = merge(same + across, cross + pair_recv[1:2, :])
-    scaled = keep / jnp.sqrt(sums)
+    scaled = keep * lax.rsqrt(sums)
     column[...] = to_column(scaled)
     mirror(1)
     landed(same_all.at[pl.ds(0, owners - 1)], same_sem.at[1])
     landed(cross_all.at[pl.ds(0, owners - 1)], cross_sem.at[1])
-    scaled_all[pl.ds(0, owners), :] = keep_all[pl.ds(0, owners), :] / jnp.sqrt(same_all[...] + cross_all[...])
+    scaled_all[pl.ds(0, owners), :] = keep_all[pl.ds(0, owners), :] * lax.rsqrt(same_all[...] + cross_all[...])
     factors = gather(scaled_all)
     form = products[1] * factors[1]
     for tile in range(2, count):
@@ -276,11 +276,10 @@
         functools.partial(kernel, owners, lax.axis_size("blk"), reach, slots, float(valid)),
         out_shape=(jax.ShapeDtypeStruct((1, block), f32),) * 3,
         out_specs=(vmem,) * 3,
-        in_specs=[hbm] * 5,
+        in_specs=[hbm, hbm, pl.BlockSpec(memory_space=pltpu.SMEM), hbm, hbm],
         scratch_shapes=[
             pltpu.SMEM(masked.shape, jnp.int32),
             pltpu.SMEM((2, slots), jnp.int32),
-            pltpu.SMEM((1,), jnp.int32),
             pltpu.VMEM((reach + slots, block, half), f32),
             pltpu.VMEM((block, half), f32),
             pltpu.VMEM((block, half), f32),
@@ -300,7 +299,7 @@
             pltpu.VMEM((1, block), f32),
             pltpu.VMEM((2, half), f32),
             pltpu.VMEM((2 * owners, 2, half), f32),
-            dma((3,)),
+            dma((2,)),
             dma((3,)),
             dma((2,)),
             dma((2, 2)),

time: 21 us -> 21 us (level)
  no operation moved by 1% of the time
where the time goes in v4:
time: 21 us; the launch traced here: 20.9 us
  Pallas kernels  18.3 us (87%)
  between operations  1.29 us (6%)
  other arithmetic  1.25 us (6%)
    pallas_call x1, Pallas kernels, local(): pl.pallas_call(functools.partial(kernel, owners, lax.axis_size('blk'), re...  18.3 us
    mul x1, other arithmetic, local(): return (jnp.sqrt(level / product), weight * product)  1.25 us

profile of v4, /device:TPU:0, one launch (start us, length us, event | category | flops | bytes accessed | tf_op | source)
XLA Modules:
  0.0 20.9 jit_solution(3500290143171238899)
XLA Ops:
  1.3 18.3 %shard_map.68 = (f32[1,256]{1,0:T(1,128)}, f32[1,256]{1,0:T(1,128)}, f32[1,256]{1,0:T(1,128)}) custom-call(s32[32]{0:T(128)} %masked_hbm.1, s32[2,16]{1,0:T(2,128)} %bitcast.3, s32[1]{0:T(128)S(6)} %copy.7.far_count, f32[1,8,256,128]{3,2,1,0:T(8,128)} %band.1, f32[16,256,128]{2,1,0:T(8,128)} %far_tiles.1), custom_call_target="tpu_custom_call" | custom-call | tf_op jit(solution)/shard_map/pallas_call | solution.py:275
  19.6 1.2 %fusion = (f32[1,256]{1,0:T(1,128)}, f32[1,256]{1,0:T(1,128)}) fusion(f32[1,256]{1,0:T(1,128)} %get-tuple-element.7, f32[1,256]{1,0:T(1,128)} %get-tuple-element.6, f32[1,256]{1,0:T(1,128)} %get-tuple-element.5), kind=kLoop, calls=%fused_computation.1 | loop fusion | flops 512 | bytes 5120 | tf_op jit(solution)/shard_map/mul | solution.py:315
